TPU v7x, 256 devices: a whole 4x4x8 slice. The times are simulated.
256 devices in a mesh: outer: 8 (over z_lo, core), inner: 32 (over y, x, z_hi).
Axes of the slice: x: 4, y: 4, z: 8 (z_hi: 2, z_lo: 4; z = z_hi * 4 + z_lo), core: 2. Of those that a mesh axis runs over, the one named last changes fastest.
Arguments:
- cotangent: bfloat16 [32768, 2048], P(('outer', 'inner')), may hold values from -0.5 to 0.5
- hidden: bfloat16 [32768, 8, 384], P(('outer', 'inner')), may hold values from -24 to 24
- probs: float32 [32768, 8], P(('outer', 'inner')), may hold values from 0.02 to 0.5
- expert_ids: int32 [32768, 8], P(('outer', 'inner')), may hold values from 0 to 63, all different within a row; in each aligned block of 128 rows (0 to 127, 128 to 255, ...) at most 24 rows name the same one
- secondary: bfloat16 [384, 64, 2048], P(None, 'inner'), may hold values from -0.3125 to 0.3125
- weight: float32 [384, 64, 2048], P('outer', 'inner'), may hold values from -0.3125 to 0.3125
- moment1: float32 [384, 64, 2048], P('outer', 'inner'), may hold values from -4 to 4
- moment2: float32 [384, 64, 2048], P('outer', 'inner'), may hold values from 0.05 to 2
Outputs:
- d_hidden: bfloat16 [32768, 8, 384], P(('outer', 'inner'))
- d_probs: float32 [32768, 8], P(('outer', 'inner'))
- new_weight: float32 [384, 64, 2048], P('outer', 'inner')
- new_moment1: float32 [384, 64, 2048], P('outer', 'inner')
- new_moment2: float32 [384, 64, 2048], P('outer', 'inner')
- new_secondary: bfloat16 [384, 64, 2048], P(None, 'inner')
Inputs may be any that keep to these rules, and one draw needn't show every extreme that they name: `expert_ids`: each token names 8 different experts. Among the 1024 choices of the rows of one device (aligned blocks of 128 tokens), no expert is named more than 24 times, a bound that some block reaches.
All inputs are finite; a program needn't handle non-finite values.
Results may differ from a plain program's by a relative error of at most 0.0085.
Values may be sent and summed in bfloat16 or wider, within the bound.
A program may use at most 128 MiB of HBM per device.

v0:
```python
import jax
import jax.numpy as jnp
from jax import lax
from jax.sharding import PartitionSpec as P

EXPERTS = 64
CAP = 24


beta_one = 0.9
beta_two = 0.95
adam_epsilon = 1e-08
learn_rate = 0.003
decay_rate = 0.1
bias_one = 1.0 - 0.9**20
bias_two = 1.0 - 0.95**20


def slot_targets(flat_ids):
    count = flat_ids.shape[0]
    block = 128
    blocks = count // block
    onehot = (jnp.arange(EXPERTS, dtype=jnp.int32)[:, None] == flat_ids[None, :]).astype(
        jnp.bfloat16
    )
    tiles = onehot.reshape(EXPERTS, blocks, block)
    lower = (jnp.arange(block)[:, None] < jnp.arange(block)[None, :]).astype(jnp.bfloat16)
    within = jnp.einsum("ebk,kj->ebj", tiles, lower, preferred_element_type=jnp.float32)
    totals = jnp.sum(tiles.astype(jnp.float32), axis=2)
    small = (jnp.arange(blocks)[:, None] < jnp.arange(blocks)[None, :]).astype(jnp.float32)
    before = jnp.dot(totals, small, precision=lax.Precision.HIGHEST)
    ranking = (within + before[..., None]).reshape(EXPERTS, count)
    position = jnp.sum(ranking * onehot.astype(jnp.float32), axis=0).astype(jnp.int32)
    return flat_ids * CAP + position


def local(cotangent, hidden, probs, expert_ids, secondary, weight, moment1, moment2):
    token_count = cotangent.shape[0]
    top_k = expert_ids.shape[1]
    hidden_width = hidden.shape[2]
    feature_width = cotangent.shape[1]
    local_experts = secondary.shape[1]
    group_size = lax.axis_size("inner")
    choice_count = token_count * top_k
    target = slot_targets(expert_ids.reshape(choice_count))
    all_slots = jnp.arange(EXPERTS * CAP, dtype=jnp.int32)
    matches = (all_slots[:, None] == target[None, :]).astype(jnp.bfloat16)
    weighted = (
        (probs[..., None] * hidden.astype(jnp.float32))
        .astype(jnp.bfloat16)
        .reshape(choice_count, hidden_width)
    )
    w_send = jnp.dot(matches, weighted, preferred_element_type=jnp.float32).astype(jnp.bfloat16)
    w_send = w_send.reshape(group_size, local_experts, CAP, hidden_width)
    all_cot, all_ids = (
        lax.all_gather(cotangent, "inner", axis=0, tiled=True),
        lax.all_gather(expert_ids, "inner", axis=0, tiled=True),
    )
    w_recv = lax.all_to_all(w_send, "inner", split_axis=0, concat_axis=0, tiled=True)
    source_ids = all_ids.reshape(group_size, choice_count)
    source_target = jax.vmap(slot_targets)(source_ids)
    offset = lax.axis_index("inner") * (local_experts * CAP)
    mine_slots = offset + jnp.arange(local_experts * CAP, dtype=jnp.int32)
    mine_match = (mine_slots[None, :, None] == source_target[:, None, :]).astype(jnp.bfloat16)
    token_match = jnp.sum(
        mine_match.reshape(group_size, local_experts * CAP, token_count, top_k), axis=3
    )
    cot_blocks = all_cot.reshape(group_size, token_count, feature_width)
    d_recv = jnp.einsum(
        "jst,jtd->jsd", token_match, cot_blocks, preferred_element_type=jnp.float32
    ).astype(jnp.bfloat16)
    d_recv = d_recv.reshape(group_size, local_experts, CAP, feature_width)
    grads = jnp.einsum(
        "jlcd,hld->jlch", d_recv, secondary, preferred_element_type=jnp.float32
    ).astype(jnp.bfloat16)
    grad = lax.psum_scatter(
        jnp.einsum("jlch,jlcd->hld", w_recv, d_recv, preferred_element_type=jnp.float32).astype(
            jnp.bfloat16
        ),
        "outer",
        scatter_dimension=0,
        tiled=True,
    ).astype(jnp.float32)
    back = lax.all_to_all(grads, "inner", split_axis=0, concat_axis=0, tiled=True)
    back = back.reshape(group_size * local_experts * CAP, hidden_width)
    g_rows = back[target].astype(jnp.float32).reshape(token_count, top_k, hidden_width)
    d_hidden = (probs[..., None] * g_rows).astype(jnp.bfloat16)
    d_probs = jnp.sum(hidden.astype(jnp.float32) * g_rows, axis=-1)
    new_moment1 = beta_one * moment1 + (1.0 - beta_one) * grad
    new_moment2 = beta_two * moment2 + (1.0 - beta_two) * grad * grad
    update = (
        new_moment1 / bias_one / (jnp.sqrt(new_moment2 / bias_two) + adam_epsilon)
        + decay_rate * weight
    )
    new_weight = weight - learn_rate * update
    new_secondary = lax.all_gather(new_weight.astype(jnp.bfloat16), "outer", axis=0, tiled=True)
    return (d_hidden, d_probs, new_weight, new_moment1, new_moment2, new_secondary)


def solution(mesh):
    in_specs = (
        P(("outer", "inner"), None),
        P(("outer", "inner"), None, None),
        P(("outer", "inner"), None),
        P(("outer", "inner"), None),
        P(None, "inner", None),
        P("outer", "inner", None),
        P("outer", "inner", None),
        P("outer", "inner", None),
    )
    out_specs = (
        P(("outer", "inner"), None, None),
        P(("outer", "inner"), None),
        P("outer", "inner", None),
        P("outer", "inner", None),
        P("outer", "inner", None),
        P(None, "inner", None),
    )
    return jax.shard_map(local, mesh=mesh, in_specs=in_specs, out_specs=out_specs, check_vma=False)
```

profile of v0, /device:TPU:1, one launch (start us, length us, event | category | flops | bytes accessed | tf_op | source)
XLA Modules:
  0.0 497.7 jit_solution(12514745437991008625)
XLA Ops:
  7.2 0.0 all-gather.3.cloned.1.call-start
  7.2 0.7 all-gather.3.cloned.1.call-update
  7.9 1.0 copy.112
  8.9 0.1 eq.71
  9.0 0.7 broadcast_multiply_fusion
  9.7 0.1 copy.111
  9.8 0.1 mul.111
  9.9 0.8 copy.102
  10.7 0.1 convert_reduce_fusion.1
  10.8 0.1 fusion.38
  11.0 0.2 fusion.26
  11.2 4.1 fusion.11
  15.3 14.6 %all-to-all-start.1 = ((bf16[32,2,24,384]{3,2,1,0:T(8,128)(2,1)}), bf16[32,2,24,384]{3,2,1,0:T(8,128)(2,1)}, u32[]{:S(2)}, u32[]{:S(2)}) async-start(bf16[32,2,24,384]{3,2,1,0:T(8,128)(2,1)} %bitcast.50), calls=%async_computation.1 | async-start | bytes 2359296 | tf_op jit(solution)/shard_map/all_to_all | solution.py:59
  29.9 0.0 all-reduce.3.cloned.1.call-start
  30.0 137.1 %all_gather.9 = s32[4096,8]{0,1:T(8,128)S(1)} all-gather(s32[128,8]{0,1:T(8,128)S(1)} %copy-done.6), channel_id=1, replica_groups=mesh['outer'=8,'inner'=32] {'inner'}, dimensions={0}, use_global_device_ids=true | all-gather | bytes 135168 | tf_op jit(solution)/shard_map/all_gather | solution.py:57
  167.1 1.9 copy.103
  169.0 2.6 eq.65
  171.7 2.2 convert_reduce_fusion
  173.9 0.6 fusion.40
  174.5 3.1 fusion
  177.6 1.0 copy.106
  178.6 1.2 copy.107
  179.9 2.6 fusion.7
  182.5 100.9 %all-gather.3.cloned.1.call-done = bf16[4096,2048]{1,0:T(8,128)(2,1)} async-done(((bf16[128,2048]{1,0:T(8,128)(2,1)}), bf16[4096,2048]{1,0:T(8,128)(2,1)}) %all-gather.3.cloned.1.call-update) | async-done | bytes 16777232 | tf_op jit(solution)/shard_map/all_gather | solution.py:56
  283.4 10.7 %convolution_convert_fusion = bf16[32,48,2048]{2,1,0:T(8,128)(2,1)} fusion(bf16[32,48,128]{2,1,0:T(8,128)(2,1)S(1)} %fusion.7, bf16[32,128,2048]{2,1,0:T(8,128)(2,1)} %bitcast.46), kind=kOutput, calls=%fused_computation.13 | convolution fusion | flops 808452096 | bytes 23461888 | tf_op jit(solution)/shard_map/jst,jtd->jsd/dot_general | solution.py:69
  294.1 8.2 %fusion.10 = bf16[384,2,2048]{0,2,1:T(8,128)(2,1)} fusion(bf16[32,2,24,2048]{3,2,1,0:T(8,128)(2,1)} %bitcast.47, bf16[32,2,24,384]{3,2,1,0:T(8,128)(2,1)} %all-to-all-done.1), kind=kOutput, calls=%fused_computation.18 | convolution fusion | flops 2417491968 | bytes 10616832 | tf_op jit(solution)/shard_map/jlch,jlcd->hld/dot_general | solution.py:77
  302.3 8.7 %copy.116 = bf16[384,2,2048]{2,1,0:T(2,128)(2,1)} copy(bf16[384,2,2048]{0,2,1:T(8,128)(2,1)} %fusion.10) | data formatting | bytes 6291456 | tf_op jit(solution)/shard_map/convert_element_type | solution.py:77
  311.0 0.0 all-reduce.3.cloned.1.call-update
  311.1 0.3 all-gather.5.cloned.1.call-start
  311.3 0.4 copy-done.7
  311.7 0.6 dynamic-slice
  312.9 82.8 %all-reduce.3.cloned.1.call-done = bf16[384,2,2048]{2,1,0:T(2,128)(2,1)} async-done(((bf16[384,2,2048]{2,1,0:T(2,128)(2,1)}), bf16[384,2,2048]{2,1,0:T(2,128)(2,1)}) %all-reduce.3.cloned.1.call-update) | async-done | bytes 3145744
  395.7 1.3 constant_dynamic-slice_fusion
  397.0 4.6 fusion.42
  401.6 1.2 copy.121
  402.8 0.0 all-gather.5.cloned.1.call-update
  402.8 6.5 %fusion.20 = bf16[32,2,24,384]{3,2,0,1:T(8,128)(2,1)S(1)} fusion(bf16[384,2,2048,1]{2,1,0,3:T(2,128)(2,1)S(1)} %bitcast.45, bf16[32,2,24,2048]{3,2,1,0:T(8,128)(2,1)} %bitcast.48), kind=kOutput, calls=%fused_computation.27 | convolution fusion | flops 2416508928 | bytes 10616832 | tf_op jit(solution)/shard_map/jlcd,hld->jlch/dot_general | solution.py:73
  409.3 1.1 copy.110
  410.5 11.2 %all-to-all-start = ((bf16[32,2,24,384]{3,2,1,0:T(8,128)(2,1)}), bf16[32,2,24,384]{3,2,1,0:T(8,128)(2,1)}, u32[]{:S(2)}, u32[]{:S(2)}) async-start(bf16[32,2,24,384]{3,2,1,0:T(8,128)(2,1)} %copy.110), calls=%async_computation | async-start | bytes 2359296 | tf_op jit(solution)/shard_map/all_to_all | solution.py:84
  421.7 0.1 mul.105
  421.8 47.2 %all-to-all-done = bf16[32,2,24,384]{3,2,1,0:T(8,128)(2,1)} async-done(((bf16[32,2,24,384]{3,2,1,0:T(8,128)(2,1)}), bf16[32,2,24,384]{3,2,1,0:T(8,128)(2,1)}, u32[]{:S(2)}, u32[]{:S(2)}) %all-to-all-start) | async-done | bytes 1179680 | tf_op jit(solution)/shard_map/all_to_all | solution.py:84
  469.0 6.3 %gather_fusion = bf16[1024,384]{1,0:T(8,128)(2,1)} fusion(bf16[1536,384]{1,0:T(8,128)(2,1)} %bitcast.9, s32[1024]{0:T(1024)S(1)} %broadcast_clamp_fusion), kind=kCustom, calls=%fused_computation | custom fusion | bytes 1576960 | tf_op jit(solution)/shard_map/gather | solution.py:86
  475.4 2.6 fusion.14
  478.0 0.7 copy.122
  478.7 2.7 copy.123
  481.4 2.6 copy.124
  484.0 1.5 copy.125
  485.5 5.7 %copy.161 = bf16[384,2,2048]{2,1,0:T(2,128)(2,1)} copy(bf16[384,2,2048]{2,1,0:T(2,128)(2,1)} %all-gather.5.cloned.1.call-done) | data formatting | bytes 6291456
  (24 shorter events, 0.1 us)
Async XLA Ops:
  7.2 395.7 %copy-start = (bf16[384,2,2048]{2,1,0:T(2,128)(2,1)S(1)}, bf16[384,2,2048]{2,1,0:T(2,128)(2,1)}, u32[]{:S(2)}) copy-start(bf16[384,2,2048]{2,1,0:T(2,128)(2,1)} %param.12) | copy-start | bytes 9437188
  7.2 276.2 %all-gather.3.cloned.1.call-start = ((), (), s32[]{:S(2)}) async-start(), calls=%async_computation.2 | async-start | bytes 17301504 | tf_op jit(solution)/shard_map/all_gather | solution.py:56
  9.8 5.5 %copy-start.2 = (s32[128,8]{1,0:T(8,128)}, s32[128,8]{1,0:T(8,128)S(1)}, u32[]{:S(2)}) copy-start(s32[128,8]{1,0:T(8,128)S(1)} %copy.111) | copy-start | bytes 12292
  10.7 4.6 copy-start.4
  11.2 18.8 %copy-start.6 = (s32[128,8]{0,1:T(8,128)S(1)}, s32[128,8]{0,1:T(8,128)}, u32[]{:S(2)}) copy-start(s32[128,8]{0,1:T(8,128)} %param.11) | copy-start | bytes 12292
  15.3 278.8 %all-to-all-start.1 = ((bf16[32,2,24,384]{3,2,1,0:T(8,128)(2,1)}), bf16[32,2,24,384]{3,2,1,0:T(8,128)(2,1)}, u32[]{:S(2)}, u32[]{:S(2)}) async-start(bf16[32,2,24,384]{3,2,1,0:T(8,128)(2,1)} %bitcast.50), calls=%async_computation.1 | async-start | bytes 2359296 | tf_op jit(solution)/shard_map/all_to_all | solution.py:59
  29.9 365.8 %all-reduce.3.cloned.1.call-start = ((), (), s32[]{:S(2)}) async-start(), calls=%async_computation.4 | async-start | bytes 6291456
  311.0 0.7 copy-start.7
  311.1 174.4 %all-gather.5.cloned.1.call-start = ((), (), s32[]{:S(2)}) async-start(), calls=%async_computation.3 | async-start | bytes 3538944 | tf_op jit(solution)/shard_map/all_gather | solution.py:96
  409.3 12.3 %copy-start.3 = (s32[128,8]{1,0:T(8,128)S(1)}, s32[128,8]{1,0:T(8,128)}, u32[]{:S(2)}) copy-start(s32[128,8]{1,0:T(8,128)} %copy-done.2) | copy-start | bytes 12292
  410.5 58.6 %all-to-all-start = ((bf16[32,2,24,384]{3,2,1,0:T(8,128)(2,1)}), bf16[32,2,24,384]{3,2,1,0:T(8,128)(2,1)}, u32[]{:S(2)}, u32[]{:S(2)}) async-start(bf16[32,2,24,384]{3,2,1,0:T(8,128)(2,1)} %copy.110), calls=%async_computation | async-start | bytes 2359296 | tf_op jit(solution)/shard_map/all_to_all | solution.py:84
  469.0 6.3 %copy-start.5 = (f32[128,8]{1,0:T(8,128)S(1)}, f32[128,8]{1,0:T(8,128)}, u32[]{:S(2)}) copy-start(f32[128,8]{1,0:T(8,128)} %copy-done.4) | copy-start | bytes 12292
  478.7 5.3 %copy-start.1 = (f32[48,2,2048]{2,0,1:T(8,128)S(1)}, f32[48,2,2048]{2,0,1:T(8,128)}, u32[]{:S(2)}) copy-start(f32[48,2,2048]{2,0,1:T(8,128)} %get-tuple-element.45) | copy-start | bytes 2359300
Sparse Core Ops, SparseCore 0:
  11.4 271.8 all-gather.2
  311.2 84.4 all-reduce.2
  402.9 67.7 all-gather.4
where the time goes:
time: 499 us; the launch traced here: 498 us
  waiting for transfers between devices  232 us (46%)
  blocking collectives  137 us (27%)
  local copies, waits for them, and re-layouts  41.7 us (8%)
  matrix products  33.6 us (7%)
  starting transfers between devices  26.1 us (5%)
  between operations  14.6 us (3%)
  other arithmetic  13 us (3%)
    all_gather x1, blocking collectives, local(): lax.all_gather(expert_ids, 'inner', axis=0, tiled=True)  137 us
    all_gather x1, waiting for transfers between devices, local(): lax.all_gather(cotangent, 'inner', axis=0, tiled=True)  101 us
    unnamed x4, waiting for transfers between devices  83.5 us
    all_to_all x1, waiting for transfers between devices, local(): lax.all_to_all(grads, 'inner', split_axis=0, concat_axis=0, tiled=True)  47.2 us
    unnamed x25, local copies, waits for them, and re-layouts  17.2 us
    all_to_all x1, starting transfers between devices, local(): lax.all_to_all(w_send, 'inner', split_axis=0, concat_axis=0, tiled=True)  14.6 us
    all_to_all x1, starting transfers between devices, local(): lax.all_to_all(grads, 'inner', split_axis=0, concat_axis=0, tiled=True)  11.2 us
    dot_general x1, matrix products, local(): jnp.einsum('jst,jtd->jsd', token_match, cot_blocks, preferred_element_typ...  10.7 us
  transfers between devices with their start and end apart: 5, of which 3 were waited for; matrix products, arithmetic and copies ran while one was open for 12% of the time, Pallas kernels for 0%

commit v1 on v0

v1 whole, which is shorter than its diff:
```python
import functools

import jax
import jax.numpy as jnp
from jax import lax
from jax.experimental import pallas as pl
from jax.experimental.pallas import tpu as pltpu
from jax.sharding import PartitionSpec as P

EXPERTS = 64
CAP = 24
H = 384
D = 2048
NC = 4
CW = D // NC
MESH = pl.DeviceIdType.MESH
F32 = jnp.float32
BF16 = jnp.bfloat16

beta_one = 0.9
beta_two = 0.95
adam_epsilon = 1e-08
learn_rate = 0.003
decay_rate = 0.1
bias_one = 1.0 - 0.9**20
bias_two = 1.0 - 0.95**20


def body(
    cot_hbm, wsend, psend, sec_hbm, weight, moment1, moment2, tcol, pcol, hid,
    dh, dp, nw, nm1, nm2, ns,
    cot, sec, posr, wr, G, wT, M2, dsl, Pb, Ps, Rr, bs, br, TT, wv, m1v, m2v, nsv,
    loc, pos_s, pos_r, w_s, w_r, b_s, b_r, ag_s, ag_r, sc_s, sc_r, sd_s, sd_r,
    pd_s, pd_r, rs_s, rs_r, z_s, z_r, y_s, y_r,
):
    o = lax.axis_index("outer")
    i = lax.axis_index("inner")
    k = lax.rem(o, 2)
    zl = lax.div(o, 2)
    zh = lax.rem(i, 2)
    own = lax.div(i, 2)
    x = lax.rem(own, 4)
    y = lax.div(own, 4)
    z = zh * 4 + zl

    def dev(px, py, pz, pk):
        return (lax.rem(pz, 4) * 2 + pk, (py * 4 + px) * 2 + lax.div(pz, 4))

    def plane(p):
        return (o, p * 2 + zh)

    xp, xm = lax.rem(x + 1, 4), lax.rem(x + 3, 4)
    yp, ym = lax.rem(y + 1, 4), lax.rem(y + 3, 4)
    zp, zm = lax.rem(z + 1, 8), lax.rem(z + 7, 8)
    dxp, dxm = dev(xp, y, z, k), dev(xm, y, z, k)
    dyp, dym = dev(x, yp, z, k), dev(x, ym, z, k)
    dzp, dzm = dev(x, y, zp, k), dev(x, y, zm, k)
    sib = (zl * 2 + 1 - k, i)

    def remote(src, dst, ss, rs, where):
        return pltpu.make_async_remote_copy(
            src_ref=src, dst_ref=dst, send_sem=ss, recv_sem=rs, device_id=where, device_id_type=MESH
        )

    barrier = pltpu.get_barrier_semaphore()

    def hello(r, c):
        pl.semaphore_signal(
            barrier, inc=1, device_id=plane(lax.rem(own + r, 16)), device_id_type=MESH
        )
        return c

    lax.fori_loop(1, 16, hello, 0)
    for r in (1, 2, 3):
        pl.semaphore_signal(
            barrier, inc=1, device_id=(lax.rem(zl + r, 4) * 2 + k, i), device_id_type=MESH
        )
    for where in (sib, dzp, dzm):
        pl.semaphore_signal(barrier, inc=1, device_id=where, device_id_type=MESH)

    locals_ = [
        pltpu.make_async_copy(cot_hbm, cot.at[y, x], loc.at[0]),
        pltpu.make_async_copy(sec_hbm, sec.at[pl.ds(zh * 2, 2)], loc.at[1]),
        pltpu.make_async_copy(wsend.at[own], wr.at[own], loc.at[2]),
        pltpu.make_async_copy(psend.at[own], posr.at[own], loc.at[3]),
        pltpu.make_async_copy(weight, wv, loc.at[4]),
        pltpu.make_async_copy(moment1, m1v, loc.at[5]),
        pltpu.make_async_copy(moment2, m2v, loc.at[6]),
    ]
    for cp in locals_:
        cp.start()
    pl.semaphore_wait(barrier, 21)

    def cols(c):
        return pl.ds(c * CW, CW)

    def pos_copy(r, p):
        return remote(psend.at[p], posr.at[own], pos_s.at[r], pos_r.at[r], plane(p))

    def w_copy(r, p):
        return remote(wsend.at[p], wr.at[own], w_s.at[r], w_r.at[r], plane(p))

    def back_copy(r, p):
        return remote(bs.at[p], br.at[own], b_s.at[r], b_r.at[r], plane(p))

    A, B = pl.ds(0, 64), pl.ds(64, 64)
    A0, A1, B0, B1 = pl.ds(0, 32), pl.ds(32, 32), pl.ds(64, 32), pl.ds(96, 32)

    def gather_send(c, n):
        q = cols(c)
        spec = (
            (cot_hbm.at[A, q], cot.at[y, x, A, q], dxp),
            (cot_hbm.at[A, q], cot.at[y, x, A, q], dxm),
            (cot_hbm.at[B, q], cot.at[y, x, B, q], dyp),
            (cot_hbm.at[B, q], cot.at[y, x, B, q], dym),
            (cot.at[y, xm, A0, q],) * 2 + (dxp,),
            (cot.at[y, xp, A1, q],) * 2 + (dxm,),
            (cot.at[ym, x, B0, q],) * 2 + (dyp,),
            (cot.at[yp, x, B1, q],) * 2 + (dym,),
            (cot.at[y, :, A, q],) * 2 + (dyp,),
            (cot.at[y, :, A, q],) * 2 + (dym,),
            (cot.at[:, x, B, q],) * 2 + (dxp,),
            (cot.at[:, x, B, q],) * 2 + (dxm,),
            (cot.at[ym, :, A0, q],) * 2 + (dyp,),
            (cot.at[yp, :, A1, q],) * 2 + (dym,),
            (cot.at[:, xm, B0, q],) * 2 + (dxp,),
            (cot.at[:, xp, B1, q],) * 2 + (dxm,),
        )[n]
        return remote(spec[0], spec[1], ag_s.at[c, n], ag_r.at[c, n], spec[2])

    def g_start(c, stage):
        for n in range(4 * stage, 4 * stage + 4):
            gather_send(c, n).start()

    def g_wait(c, stage):
        for n in range(4 * stage, 4 * stage + 4):
            gather_send(c, n).wait_recv()

    q_up = 1 - lax.div(zp, 4)
    q_dn = 1 - lax.div(zm, 4)
    other = 1 - zh
    R0_, R1_ = pl.ds(0, 192), pl.ds(192, 192)

    def chain(c, way):
        q = cols(c)
        ref = sec.at[q_up * 2 + k, R0_, q] if way == 0 else sec.at[q_dn * 2 + k, R1_, q]
        return remote(ref, ref, sc_s.at[c, way], sc_r.at[c, way], dzp if way == 0 else dzm)

    def chain_sib(c, way):
        ref = sec.at[other * 2 + k, R0_ if way == 0 else R1_, cols(c)]
        return remote(ref, ref, sd_s.at[c, way], sd_r.at[c, way], sib)

    def chain_begin():
        locals_[1].wait()

        @pl.when(zl == 3)
        def _():
            for c in range(NC):
                chain(c, 0).start()

        @pl.when(zl == 0)
        def _():
            for c in range(NC):
                chain(c, 1).start()

    def chain_step(c):
        chain(c, 0).wait_recv()

        @pl.when(zl < 3)
        def _():
            chain(c, 0).start()

        chain_sib(c, 0).start()
        chain(c, 1).wait_recv()

        @pl.when(zl > 0)
        def _():
            chain(c, 1).start()

        chain_sib(c, 1).start()

    def chain_end(c):
        chain_sib(c, 0).wait_recv()
        chain_sib(c, 1).wait_recv()

    def build_TT():
        def one(b, carry):
            rows = pl.ds(b * 128, 128)
            t = tcol[rows, :]
            slot = lax.broadcasted_iota(jnp.int32, (128, EXPERTS * CAP), 1)
            TT[rows, :] = jnp.where(slot == t, 1.0, 0.0).astype(BF16)
            return carry

        lax.fori_loop(0, 8, one, 0)

    def build_M2():
        def one(b, carry):
            j = lax.broadcasted_iota(jnp.int32, (CAP, 128), 0).astype(F32)
            zero = jnp.zeros((CAP, 128), F32)
            first, second = posr[2 * b], posr[2 * b + 1]
            rows = []
            for q in range(4):
                one_a = jnp.where(first[q : q + 1, :] == j, 1.0, 0.0)
                one_b = jnp.where(second[q : q + 1, :] == j, 1.0, 0.0)
                rows.append(jnp.concatenate([one_a, zero], axis=1))
                rows.append(jnp.concatenate([zero, one_b], axis=1))
            M2[b] = jnp.concatenate(rows, axis=0).astype(BF16)
            return carry

        lax.fori_loop(0, 8, one, 0)

    def build_wT():
        def one(s, carry):
            block = wr[s].astype(F32)
            for q in range(4):
                G[q, pl.ds(s * CAP, CAP), :] = block[q * CAP : (q + 1) * CAP, :]
            return carry

        lax.fori_loop(0, 16, one, 0)
        for q in range(4):
            wT[q] = jnp.transpose(G[q]).astype(BF16)

    def rows_of(c):
        q = cols(c)

        def one(b, carry):
            block = cot[lax.div(b, 2), pl.ds(lax.rem(b, 2) * 2, 2), :, q].reshape(256, CW)
            got = jnp.dot(M2[b], block, preferred_element_type=F32).astype(BF16)
            for e in range(4):
                dsl[e, pl.ds(b * 48, 48), :] = got[e * 48 : (e + 1) * 48, :]
            return carry

        lax.fori_loop(0, 8, one, 0)

    def partials(c):
        for e in range(4):
            got = jnp.dot(wT[e], dsl[e], preferred_element_type=F32).astype(BF16)
            for s in range(8):
                Pb[c, s % 2, (e // 2) * 4 + s // 2, e % 2] = got[s * 48 : (s + 1) * 48, :]

    def hidden_grads(c):
        for e in range(4):
            got = lax.dot_general(
                dsl[e], sec[e, :, cols(c)], (((1,), (1,)), ((), ())), preferred_element_type=F32
            )
            G[e] = got if c == 0 else G[e] + got

    def pair_copy(c):
        return remote(Pb.at[c, 1 - k], Ps.at[c], pd_s.at[c], pd_r.at[c], sib)

    def ring_copy(c, t, way):
        far = 4 - t
        d = lax.rem(z + far, 8) if way == 0 else lax.rem(z + 8 - far, 8)
        where = dzp if way == 0 else dzm
        if t == 0:
            src, dst = Pb.at[c, k, d, way], Rr.at[c, t, way, way]
        else:
            src, dst = Pb.at[c, k, d], Rr.at[c, t, way]
        return remote(src, dst, rs_s.at[c, t, way], rs_r.at[c, t, way], where)

    def pair_sum(c):
        pair_copy(c).wait_recv()
        Pb[c, k] = (Pb[c, k].astype(F32) + Ps[c].astype(F32)).astype(BF16)
        ring_copy(c, 0, 0).start()
        ring_copy(c, 0, 1).start()

    def ring_step(c, t):
        for way in range(2):
            far = 4 - t
            d = lax.rem(z + far, 8) if way == 0 else lax.rem(z + 8 - far, 8)
            ring_copy(c, t - 1, way).wait_recv()
            if t == 1:
                Pb[c, k, d, way] = (
                    Pb[c, k, d, way].astype(F32) + Rr[c, 0, way, way].astype(F32)
                ).astype(BF16)
            else:
                Pb[c, k, d] = (Pb[c, k, d].astype(F32) + Rr[c, t - 1, way].astype(F32)).astype(BF16)
            ring_copy(c, t, way).start()

    def z_copy(c, r):
        src = nsv.at[:, :, cols(c)]
        dst = ns.at[2 * zl + k, :, :, cols(c)]
        return remote(src, dst, z_s.at[c, r], z_r.at[c, r], (lax.rem(zl + r, 4) * 2 + k, i))

    def y_copy(c, r):
        home = 2 * lax.rem(zl + 4 - r, 4) + k
        dst = ns.at[home, :, :, cols(c)]
        src = nsv.at[:, :, cols(c)] if r == 0 else dst
        return remote(src, dst, y_s.at[c, r], y_r.at[c, r], sib)

    def own_copy(c):
        return pltpu.make_async_copy(
            nsv.at[:, :, cols(c)], ns.at[2 * zl + k, :, :, cols(c)], loc.at[7 + c]
        )

    def out_copies(c):
        q = cols(c)
        return [
            pltpu.make_async_copy(v.at[:, :, q], dst.at[:, :, q], loc.at[7 + NC + 3 * c + n])
            for n, (v, dst) in enumerate(((wv, nw), (m1v, nm1), (m2v, nm2)))
        ]

    def adam(c):
        q = cols(c)
        if c == 0:
            for cp in locals_[4:]:
                cp.wait()
        ring_copy(c, 3, 0).wait_recv()
        ring_copy(c, 3, 1).wait_recv()
        grad = Pb[c, k, z].astype(F32) + Rr[c, 3, 0].astype(F32) + Rr[c, 3, 1].astype(F32)
        w = wv[:, :, q]
        a = beta_one * m1v[:, :, q] + (1.0 - beta_one) * grad
        b = beta_two * m2v[:, :, q] + (1.0 - beta_two) * grad * grad
        update = a / bias_one / (jnp.sqrt(b / bias_two) + adam_epsilon) + decay_rate * w
        w = w - learn_rate * update
        wv[:, :, q] = w
        m1v[:, :, q] = a
        m2v[:, :, q] = b
        nsv[:, :, q] = w.astype(BF16)
        for r in (1, 2, 3):
            z_copy(c, r).start()
        y_copy(c, 0).start()
        own_copy(c).start()
        for cp in out_copies(c):
            cp.start()

    def z_forward(c):
        for r in (1, 3, 2):
            z_copy(c, r).wait_recv()
            y_copy(c, r).start()

    def z_end(c):
        for r in range(4):
            y_copy(c, r).wait_recv()

    def send_back():
        def one(r, carry):
            s = lax.rem(own + r, 16)
            rows = [G[e, pl.ds(s * CAP, CAP), :] for e in range(4)]
            bs[s] = jnp.concatenate(rows, axis=0).astype(BF16)

            @pl.when(r < 16)
            def _():
                back_copy(r, s).start()

            return carry

        lax.fori_loop(1, 17, one, 0)
        pltpu.make_async_copy(bs.at[own], br.at[own], loc.at[7 + 4 * NC]).start()

    def finish():
        pltpu.make_async_copy(bs.at[own], br.at[own], loc.at[7 + 4 * NC]).wait()

        def arrive(r, carry):
            p = lax.rem(own + 16 - r, 16)
            remote(br.at[p], br.at[p], b_s.at[r], b_r.at[r], plane(p)).wait_recv()
            return carry

        lax.fori_loop(1, 16, arrive, 0)

        def one(b, carry):
            rows = pl.ds(b * 128, 128)
            g = jnp.dot(
                TT[rows, :], br[...].reshape(EXPERTS * CAP, H), preferred_element_type=F32
            )
            dh[rows, :] = (pcol[rows, :] * g).astype(BF16)
            dp[rows, :] = jnp.sum(hid[rows, :].astype(F32) * g, axis=1, keepdims=True)
            return carry

        lax.fori_loop(0, 8, one, 0)

    def send_rows(r, carry):
        p = lax.rem(own + r, 16)
        pos_copy(r, p).start()
        w_copy(r, p).start()
        return carry

    def pos_arrive(r, carry):
        p = lax.rem(own + 16 - r, 16)
        remote(posr.at[p], posr.at[p], pos_s.at[r], pos_r.at[r], plane(p)).wait_recv()
        return carry

    def w_arrive(r, carry):
        p = lax.rem(own + 16 - r, 16)
        remote(wr.at[p], wr.at[p], w_s.at[r], w_r.at[r], plane(p)).wait_recv()
        return carry

    g_start(0, 0)
    lax.fori_loop(1, 16, send_rows, 0)
    chain_begin()
    for c in range(1, NC):
        g_start(c, 0)
    build_TT()
    locals_[0].wait()
    g_wait(0, 0)
    g_start(0, 1)
    g_wait(0, 1)
    g_start(0, 2)
    lax.fori_loop(1, 16, pos_arrive, 0)
    locals_[3].wait()
    build_M2()
    g_wait(1, 0)
    g_start(1, 1)
    g_wait(0, 2)
    g_start(0, 3)
    g_wait(1, 1)
    g_start(1, 2)
    chain_step(0)
    lax.fori_loop(1, 16, w_arrive, 0)
    locals_[2].wait()
    build_wT()

    for c in range(NC):
        g_wait(c, 3)
        rows_of(c)
        if c + 2 < NC:
            g_wait(c + 2, 0)
            g_start(c + 2, 1)
        partials(c)
        pair_copy(c).start()
        if c + 1 < NC:
            g_wait(c + 1, 2)
            g_start(c + 1, 3)
            chain_step(c + 1)
        if c + 2 < NC:
            g_wait(c + 2, 1)
            g_start(c + 2, 2)
        if c >= 1:
            ring_step(c - 1, 1)
        chain_end(c)
        hidden_grads(c)
        if c == NC - 1:
            send_back()
        if c >= 1:
            ring_step(c - 1, 2)
        if c >= 2:
            adam(c - 2)
        pair_sum(c)
        if c >= 1:
            ring_step(c - 1, 3)
        if c >= 3:
            z_forward(c - 3)
    c = NC - 1
    ring_step(c, 1)
    adam(c - 1)
    ring_step(c, 2)
    z_forward(c - 2)
    ring_step(c, 3)
    z_forward(c - 1)
    adam(c)
    finish()
    z_forward(c)
    for c in range(NC):
        z_end(c)

    def sent(r, carry):
        p = lax.rem(own + r, 16)
        pos_copy(r, p).wait_send()
        w_copy(r, p).wait_send()
        back_copy(r, p).wait_send()
        return carry

    lax.fori_loop(1, 16, sent, 0)
    for c in range(NC):
        for n in range(16):
            gather_send(c, n).wait_send()
        for way in range(2):
            chain_sib(c, way).wait_send()
            for t in range(4):
                ring_copy(c, t, way).wait_send()
        chain(c, 0).wait_send()
        chain(c, 1).wait_send()
        pair_copy(c).wait_send()
        for r in range(4):
            if r:
                z_copy(c, r).wait_send()
            y_copy(c, r).wait_send()
        own_copy(c).wait()
        for cp in out_copies(c):
            cp.wait()


def slot_targets(expert_ids):
    experts = jnp.arange(EXPERTS, dtype=jnp.int32)
    ids = expert_ids.T
    chosen = jnp.any(ids[:, None, :] == experts[None, :, None], axis=0)
    before = (jnp.arange(128)[:, None] < jnp.arange(128)[None, :]).astype(BF16)
    rank = jnp.dot(chosen.astype(BF16), before, preferred_element_type=F32)
    pos = jnp.where(chosen, rank, -1.0)
    place = rank + (experts * CAP).astype(F32)[:, None]
    target = jnp.sum(
        jnp.where(ids[:, None, :] == experts[None, :, None], place[None], 0.0), axis=1
    )
    return pos, target.T.astype(jnp.int32).reshape(1024)


def local(cotangent, hidden, probs, expert_ids, secondary, weight, moment1, moment2):
    pos, target = slot_targets(expert_ids)
    pcol = probs.reshape(1024, 1)
    hid = hidden.reshape(1024, H)
    weighted = (pcol * hid.astype(F32)).astype(BF16)
    slots = jnp.arange(EXPERTS * CAP, dtype=jnp.int32)
    matches = (slots[:, None] == target[None, :]).astype(BF16)
    wsend = jnp.dot(matches, weighted, preferred_element_type=F32).astype(BF16)
    wsend = wsend.reshape(16, 4 * CAP, H)
    psend = jnp.concatenate([pos.reshape(16, 4, 128), jnp.zeros((16, 4, 128), F32)], axis=1)
    tcol = target.reshape(1024, 1)
    sec = secondary.transpose(1, 0, 2)
    wt, m1, m2 = (a.transpose(1, 0, 2) for a in (weight, moment1, moment2))

    hbm = pl.BlockSpec(memory_space=pl.ANY)
    vmem = pl.BlockSpec(memory_space=pltpu.VMEM)
    dma = pltpu.SemaphoreType.DMA
    shape = jax.ShapeDtypeStruct
    dh, dp, nw, nm1, nm2, ns = pl.pallas_call(
        body,
        out_shape=(
            shape((1024, H), BF16),
            shape((1024, 1), F32),
            shape((2, 48, D), F32),
            shape((2, 48, D), F32),
            shape((2, 48, D), F32),
            shape((8, 2, 48, D), BF16),
        ),
        in_specs=[hbm] * 7 + [vmem] * 3,
        out_specs=(vmem, vmem, hbm, hbm, hbm, hbm),
        scratch_shapes=[
            pltpu.VMEM((4, 4, 128, D), BF16),
            pltpu.VMEM((4, H, D), BF16),
            pltpu.VMEM((16, 8, 128), F32),
            pltpu.VMEM((16, 4 * CAP, H), BF16),
            pltpu.VMEM((4, H, H), F32),
            pltpu.VMEM((4, H, H), BF16),
            pltpu.VMEM((8, 192, 256), BF16),
            pltpu.VMEM((4, H, CW), BF16),
            pltpu.VMEM((NC, 2, 8, 2, 48, CW), BF16),
            pltpu.VMEM((NC, 8, 2, 48, CW), BF16),
            pltpu.VMEM((NC, 4, 2, 2, 48, CW), BF16),
            pltpu.VMEM((16, 4 * CAP, H), BF16),
            pltpu.VMEM((16, 4 * CAP, H), BF16),
            pltpu.VMEM((1024, EXPERTS * CAP), BF16),
            pltpu.VMEM((2, 48, D), F32),
            pltpu.VMEM((2, 48, D), F32),
            pltpu.VMEM((2, 48, D), F32),
            pltpu.VMEM((2, 48, D), BF16),
            dma((8 + 4 * NC,)),
            dma((16,)), dma((16,)), dma((16,)), dma((16,)), dma((16,)), dma((16,)),
            dma((NC, 16)), dma((NC, 16)),
            dma((NC, 2)), dma((NC, 2)), dma((NC, 2)), dma((NC, 2)),
            dma((NC,)), dma((NC,)),
            dma((NC, 4, 2)), dma((NC, 4, 2)),
            dma((NC, 4)), dma((NC, 4)), dma((NC, 4)), dma((NC, 4)),
        ],
        compiler_params=pltpu.CompilerParams(
            collective_id=0, has_side_effects=True, vmem_limit_bytes=60 * 1024 * 1024
        ),
    )(cotangent, wsend, psend, sec, wt, m1, m2, tcol, pcol, hid)
    nw, nm1, nm2 = (a.transpose(1, 0, 2) for a in (nw, nm1, nm2))
    ns = ns.transpose(0, 2, 1, 3).reshape(H, 2, D)
    return dh.reshape(128, 8, H), dp.reshape(128, 8), nw, nm1, nm2, ns


def solution(mesh):
    in_specs = (
        P(("outer", "inner"), None),
        P(("outer", "inner"), None, None),
        P(("outer", "inner"), None),
        P(("outer", "inner"), None),
        P(None, "inner", None),
        P("outer", "inner", None),
        P("outer", "inner", None),
        P("outer", "inner", None),
    )
    out_specs = (
        P(("outer", "inner"), None, None),
        P(("outer", "inner"), None),
        P("outer", "inner", None),
        P("outer", "inner", None),
        P("outer", "inner", None),
        P(None, "inner", None),
    )
    return jax.shard_map(local, mesh=mesh, in_specs=in_specs, out_specs=out_specs, check_vma=False)
```

time: 499 us -> 276 us (0.55)
  Pallas kernels: 0 us -> 246 us
  waiting for transfers between devices: 232 us -> 0 us
  blocking collectives: 137 us -> 0 us
  matrix products: 33.6 us -> 3 us
  starting transfers between devices: 26.1 us -> 0 us
  local copies, waits for them, and re-layouts: 41.7 us -> 23.7 us
  between operations: 14.6 us -> 0.72 us
  other arithmetic: 13 us -> 2.94 us
    pallas_call x0 -> x1, Pallas kernels: none -> 246 us  [local(): pl.pallas_call(body, out_shape=(shape((1024, H), BF16), shape((1024, 1),...]
    all_gather x1 -> x0, blocking collectives: 137 us -> none  [local(): lax.all_gather(expert_ids, 'inner', axis=0, tiled=True)]
    all_gather x2 -> x0, waiting for transfers between devices: 101 us -> none  [the longest x1 101 us: local(): lax.all_gather(cotangent, 'inner', axis=0, tiled=True)]
    unnamed x4 -> x0, waiting for transfers between devices: 83.5 us -> none
    all_to_all x2 -> x0, waiting for transfers between devices: 47.3 us -> none  [the longest x1 47.2 us: local(): lax.all_to_all(grads, 'inner', split_axis=0, concat_axis=0, tiled=True)]
    dot_general x8 -> x2, matrix products: 33.6 us -> 3 us  [the longest x1 2.91 us: local(): wsend = jnp.dot(matches, weighted, preferred_element_type=F32).astype(BF16)]
    all_to_all x2 -> x0, starting transfers between devices: 25.8 us -> none  [the longest x1 14.6 us: local(): lax.all_to_all(w_send, 'inner', split_axis=0, concat_axis=0, tiled=True)]
    convert_element_type x5 -> x1, local copies, waits for them, and re-layouts: 13.2 us -> 0.1 us  [slot_targets(): return (pos, target.T.astype(jnp.int32).reshape(1024))]
  transfers between devices with their start and end apart: 5 -> 0, of which waited for: 3 -> 0; matrix products, arithmetic and copies ran while one was open for 12% -> 0% of each run, Pallas kernels for 0% -> 0%
where the time goes in v1:
time: 276 us
  Pallas kernels  246 us (89%)
  local copies, waits for them, and re-layouts  23.7 us (9%)
  matrix products  3 us (1%)
  other arithmetic  2.94 us (1%)
    pallas_call x1, Pallas kernels, local(): pl.pallas_call(body, out_shape=(shape((1024, H), BF16), shape((1024, 1),...  246 us
    unnamed x25, local copies, waits for them, and re-layouts  18.5 us

profile of v1, /device:TPU:1, one launch (start us, length us, event | category | flops | bytes accessed | tf_op | source)
XLA Modules:
  0.0 276.0 jit_solution(14365496988944589986)
XLA Ops:
  0.6 0.0 copy-start.2
  0.7 0.8 fusion.4
  1.5 0.1 broadcast_select_fusion
  1.5 0.8 select_reduce_fusion
  2.3 0.6 concatenate.3.psend
  3.0 0.1 copy.37
  3.1 0.1 eq.18
  3.2 0.8 copy.38
  3.9 0.1 mul.22
  4.0 1.0 reshape.49.pcol
  5.0 1.0 reshape_reshape.4.tcol
  6.0 2.5 copy.58
  8.5 0.0 copy-done.2
  8.5 0.0 copy-start.6
  8.5 0.0 copy-start.7
  8.5 2.9 %fusion.2 = bf16[1536,384]{1,0:T(8,128)(2,1)} fusion(s32[1024]{0:T(1024)S(1)} %eq.18, f32[1024]{0:T(1024)S(1)} %mul.22, bf16[128,8,384]{2,1,0:T(8,128)(2,1)S(1)} %copy-done.2), kind=kOutput, calls=%fused_computation.4 | convolution fusion | flops 1211301888 | bytes 1974272 | tf_op jit(solution)/shard_map/dot_general | solution.py:504
  11.4 0.0 copy-start
  11.4 0.0 copy-done.6
  11.4 0.0 copy-done.7
  11.4 2.0 copy_bitcast_fusion.1
  13.4 0.0 copy-done
  13.4 3.0 %copy.57 = bf16[384,2,2048]{2,0,1:T(8,128)(2,1)} copy(bf16[384,2,2048]{2,1,0:T(2,128)(2,1)S(1)} %copy-done) | data formatting | bytes 6291456 | tf_op args[4]
  16.5 245.6 %shard_map.127 = (bf16[1024,384]{1,0:T(8,128)(2,1)}, f32[1024,1]{1,0:T(8,128)}, f32[2,48,2048]{2,1,0:T(8,128)}, f32[2,48,2048]{2,1,0:T(8,128)}, f32[2,48,2048]{2...) custom-call(bf16[128,2048]{1,0:T(8,128)(2,1)} %cot_hbm.1, bf16[16,96,384]{2,1,0:T(8,128)(2,1)} %bitcast.31, ...), custom_call_target="tpu_custom_call" | custom-call | tf_op jit(solution)/shard_map/pallas_call | solution.py:515
  262.1 0.0 copy-start.5
  262.1 0.0 copy-start.4
  262.1 1.4 reduce
  263.5 0.1 reshape.47
  263.6 0.7 copy.48
  264.3 0.0 copy-start.1
  264.3 2.8 %copy.49 = f32[48,2,2048]{2,1,0:T(2,128)} copy(f32[48,2,2048]{2,0,1:T(8,128)} %bitcast.36) | data formatting | bytes 1572864
  267.0 0.0 copy-done.5
  267.0 1.5 copy.50
  268.5 0.0 copy-done.4
  268.5 1.5 copy.51
  270.0 0.0 copy-done.1
  270.0 0.2 copy.47
  270.2 0.0 copy-start.3
  270.3 4.9 %copy.52 = bf16[384,2,2048]{2,1,0:T(2,128)(2,1)} copy(bf16[384,2,2048]{2,0,1:T(8,128)(2,1)S(1)} %bitcast.28) | data formatting | bytes 6291456
  275.1 0.0 copy-done.3
  275.2 0.9 copy.60
  (2 shorter events, 0.0 us)
Async XLA Ops:
  0.6 7.8 %copy-start.2 = (bf16[128,8,384]{2,1,0:T(8,128)(2,1)S(1)}, bf16[128,8,384]{2,1,0:T(8,128)(2,1)}, u32[]{:S(2)}) copy-start(bf16[128,8,384]{2,1,0:T(8,128)(2,1)} %param.9) | copy-start | bytes 2359300
  8.5 2.9 %copy-start.6 = (f32[48,2,2048]{2,1,0:T(2,128)S(1)}, f32[48,2,2048]{2,1,0:T(2,128)}, u32[]{:S(2)}) copy-start(f32[48,2,2048]{2,1,0:T(2,128)} %param.15) | copy-start | bytes 2359300
  8.5 2.9 %copy-start.7 = (f32[48,2,2048]{2,1,0:T(2,128)S(1)}, f32[48,2,2048]{2,1,0:T(2,128)}, u32[]{:S(2)}) copy-start(f32[48,2,2048]{2,1,0:T(2,128)} %param.14) | copy-start | bytes 2359300
  11.4 2.1 copy-start
  262.1 4.9 %copy-start.5 = (f32[2,48,2048]{2,1,0:T(8,128)S(1)}, f32[2,48,2048]{2,1,0:T(8,128)}, u32[]{:S(2)}) copy-start(f32[2,48,2048]{2,1,0:T(8,128)} %get-tuple-element.15) | copy-start | bytes 2359300
  262.1 6.4 %copy-start.4 = (f32[2,48,2048]{2,1,0:T(8,128)S(1)}, f32[2,48,2048]{2,1,0:T(8,128)}, u32[]{:S(2)}) copy-start(f32[2,48,2048]{2,1,0:T(8,128)} %get-tuple-element.16) | copy-start | bytes 2359300
  264.3 5.8 %copy-start.1 = (bf16[8,2,48,2048]{3,2,1,0:T(8,128)(2,1)S(1)}, bf16[8,2,48,2048]{3,2,1,0:T(8,128)(2,1)}, u32[]{:S(2)}) copy-start(bf16[8,2,48,2048]{3,2,1,0:T(8,128)(2,1)} %get-tuple-element.17) | copy-start | bytes 9437188
  270.2 4.9 %copy-start.3 = (bf16[1024,384]{1,0:T(8,128)(2,1)S(1)}, bf16[1024,384]{1,0:T(8,128)(2,1)}, u32[]{:S(2)}) copy-start(bf16[1024,384]{1,0:T(8,128)(2,1)} %get-tuple-element.12) | copy-start | bytes 2359300

commit v2 on v1

v2 whole, which is shorter than its diff:
```python
import functools

import jax
import jax.numpy as jnp
from jax import lax
from jax.experimental import pallas as pl
from jax.experimental.pallas import tpu as pltpu
from jax.sharding import PartitionSpec as P

EXPERTS = 64
CAP = 24
H = 384
D = 2048
NC = 8
CW = D // NC
MESH = pl.DeviceIdType.MESH
F32 = jnp.float32
BF16 = jnp.bfloat16

beta_one = 0.9
beta_two = 0.95
adam_epsilon = 1e-08
learn_rate = 0.003
decay_rate = 0.1
bias_one = 1.0 - 0.9**20
bias_two = 1.0 - 0.95**20


def body(
    cot_hbm, ids, prT, hid_hbm, sec_hbm, weight, moment1, moment2,
    dh, dpT, nw, nm1, nm2, ns,
    cot, sec, ps, posr, ws, wr, G, wT, M2, dsl, Pb, Ps, Rr, bs, br, TT, T, Wk, hid, outf,
    tgt, tgc, pc, wv, m1v, m2v, nsx,
    loc, in_s, out_s, pos_s, pos_r, w_s, w_r, b_s, b_r, ag_s, ag_r, sc_s, sc_r, sd_s, sd_r,
    pd_s, pd_r, rs_s, rs_r, z_s, z_r, y_s, y_r,
):
    o = lax.axis_index("outer")
    i = lax.axis_index("inner")
    k = lax.rem(o, 2)
    zl = lax.div(o, 2)
    zh = lax.rem(i, 2)
    own = lax.div(i, 2)
    x = lax.rem(own, 4)
    y = lax.div(own, 4)
    z = zh * 4 + zl

    def dev(px, py, pz, pk):
        return (lax.rem(pz, 4) * 2 + pk, (py * 4 + px) * 2 + lax.div(pz, 4))

    def plane(p):
        return (o, p * 2 + zh)

    xp, xm = lax.rem(x + 1, 4), lax.rem(x + 3, 4)
    yp, ym = lax.rem(y + 1, 4), lax.rem(y + 3, 4)
    zp, zm = lax.rem(z + 1, 8), lax.rem(z + 7, 8)
    dxp, dxm = dev(xp, y, z, k), dev(xm, y, z, k)
    dyp, dym = dev(x, yp, z, k), dev(x, ym, z, k)
    dzp, dzm = dev(x, y, zp, k), dev(x, y, zm, k)
    sib = (zl * 2 + 1 - k, i)

    def remote(src, dst, ss, rs, where):
        return pltpu.make_async_remote_copy(
            src_ref=src, dst_ref=dst, send_sem=ss, recv_sem=rs, device_id=where, device_id_type=MESH
        )

    barrier = pltpu.get_barrier_semaphore()

    def hello(r, c):
        pl.semaphore_signal(
            barrier, inc=1, device_id=plane(lax.rem(own + r, 16)), device_id_type=MESH
        )
        return c

    lax.fori_loop(1, 16, hello, 0)
    for where in (sib, dzp, dzm):
        pl.semaphore_signal(barrier, inc=1, device_id=where, device_id_type=MESH)

    locals_ = [
        pltpu.make_async_copy(hid_hbm, hid, loc.at[2]),
        pltpu.make_async_copy(weight, wv, loc.at[4]),
        pltpu.make_async_copy(moment1, m1v, loc.at[5]),
        pltpu.make_async_copy(moment2, m2v, loc.at[6]),
    ]
    def cols(c):
        return pl.ds(c * CW if isinstance(c, int) else pl.multiple_of(c * CW, CW), CW)

    def cot_in(c):
        return pltpu.make_async_copy(cot_hbm.at[:, cols(c)], cot.at[y, x, c], in_s.at[0, c])

    def sec_in(c):
        return pltpu.make_async_copy(sec_hbm.at[:, :, cols(c)], sec.at[zh, c], in_s.at[1, c])

    for c in range(NC):
        cot_in(c).start()
        sec_in(c).start()
    for cp in locals_:
        cp.start()

    def rank_choices():
        named = ids[...]
        experts = lax.broadcasted_iota(jnp.int32, (EXPERTS, 128), 0)
        hits = [named[n : n + 1, :] == experts for n in range(8)]
        chosen = functools.reduce(jnp.logical_or, hits)
        first = lax.broadcasted_iota(jnp.int32, (128, 128), 0)
        second = lax.broadcasted_iota(jnp.int32, (128, 128), 1)
        before = jnp.where(first < second, 1.0, 0.0).astype(BF16)
        rank = jnp.dot(
            jnp.where(chosen, 1.0, 0.0).astype(BF16), before, preferred_element_type=F32
        )
        ps[...] = jnp.where(chosen, rank, -1.0).reshape(8, 8, 128)
        place = rank + (experts * CAP).astype(F32)
        rows = [jnp.sum(jnp.where(hit, place, 0.0), axis=0, keepdims=True) for hit in hits]
        target = jnp.concatenate(rows, axis=0)
        tgt[...] = target
        tgc[...] = jnp.transpose(target)
        pc[...] = jnp.transpose(prT[...])

    rank_choices()
    pl.semaphore_wait(barrier, 18)

    def pos_copy(r, p):
        return remote(ps.at[lax.div(p, 2)], posr.at[own], pos_s.at[r], pos_r.at[r], plane(p))

    def w_copy(r, p):
        return remote(ws.at[p], wr.at[own], w_s.at[r], w_r.at[r], plane(p))

    def back_copy(r, p):
        return remote(bs.at[p], br.at[own], b_s.at[r], b_r.at[r], plane(p))

    A, B = pl.ds(0, 64), pl.ds(64, 64)
    A0, A1, B0, B1 = pl.ds(0, 32), pl.ds(32, 32), pl.ds(64, 32), pl.ds(96, 32)

    def gather_send(c, n):
        q = cols(c)
        spec = (
            (cot_hbm.at[A, q], cot.at[y, x, c, A], dxp),
            (cot_hbm.at[A, q], cot.at[y, x, c, A], dxm),
            (cot_hbm.at[B, q], cot.at[y, x, c, B], dyp),
            (cot_hbm.at[B, q], cot.at[y, x, c, B], dym),
            (cot.at[y, xm, c, A0],) * 2 + (dxp,),
            (cot.at[y, xp, c, A1],) * 2 + (dxm,),
            (cot.at[ym, x, c, B0],) * 2 + (dyp,),
            (cot.at[yp, x, c, B1],) * 2 + (dym,),
            (cot.at[y, :, c, A],) * 2 + (dyp,),
            (cot.at[y, :, c, A],) * 2 + (dym,),
            (cot.at[:, x, c, B],) * 2 + (dxp,),
            (cot.at[:, x, c, B],) * 2 + (dxm,),
            (cot.at[ym, :, c, A0],) * 2 + (dyp,),
            (cot.at[yp, :, c, A1],) * 2 + (dym,),
            (cot.at[:, xm, c, B0],) * 2 + (dxp,),
            (cot.at[:, xp, c, B1],) * 2 + (dxm,),
        )[n]
        return remote(spec[0], spec[1], ag_s.at[c, n], ag_r.at[c, n], spec[2])

    def g_start(c, stage):
        if stage == 2:
            cot_in(c).wait()
        for n in range(4 * stage, 4 * stage + 4):
            gather_send(c, n).start()

    def g_wait(c, stage):
        for n in range(4 * stage, 4 * stage + 4):
            gather_send(c, n).wait_recv()

    q_up = 1 - lax.div(zp, 4)
    q_dn = 1 - lax.div(zm, 4)
    other = 1 - zh
    quarter = [pl.ds(pl.multiple_of((k * 2 + way) * 96, 96), 96) for way in range(2)]

    def chain(c, way):
        ref = sec.at[(q_up, q_dn)[way], c, quarter[way]]
        return remote(ref, ref, sc_s.at[c, way], sc_r.at[c, way], (dzp, dzm)[way])

    def chain_sib(c, way):
        ref = sec.at[other, c, quarter[way]]
        return remote(ref, ref, sd_s.at[c, way], sd_r.at[c, way], sib)

    def chain_begin(c):
        sec_in(c).wait()

        @pl.when(zl == 3)
        def _():
            chain(c, 0).start()

        @pl.when(zl == 0)
        def _():
            chain(c, 1).start()

    def chain_step(slot):
        up, dn = slot - zl, slot - 3 + zl

        @pl.when((up >= 0) & (up < NC))
        def _():
            chain(up, 0).wait_recv()

            @pl.when(zl < 3)
            def _():
                chain(up, 0).start()

            chain_sib(up, 0).start()

        @pl.when((dn >= 0) & (dn < NC))
        def _():
            chain(dn, 1).wait_recv()

            @pl.when(zl > 0)
            def _():
                chain(dn, 1).start()

            chain_sib(dn, 1).start()

    def chain_end(c):
        chain_sib(c, 0).wait_recv()
        chain_sib(c, 1).wait_recv()

    def choices():
        pltpu.make_async_copy(ps.at[lax.div(own, 2)], posr.at[own], loc.at[3]).start()

        def one(r, carry):
            pos_copy(r, lax.rem(own + r, 16)).start()
            return carry

        lax.fori_loop(1, 16, one, 0)

    def build_rows():
        def one(b, carry):
            rows = pl.ds(b * 128, 128)
            slot = (lax.broadcasted_iota(jnp.int32, (128, 128), 0) + b * 128).astype(F32)
            for n in range(8):
                hit = slot == tgt[n : n + 1, :]
                T[rows, n * 128 : (n + 1) * 128] = jnp.where(hit, 1.0, 0.0).astype(BF16)
            return carry

        lax.fori_loop(0, 12, one, 0)
        locals_[0].wait()
        for n in range(8):
            rows = pc[:, n : n + 1] * hid[:, n, :].astype(F32)
            Wk[n * 128 : (n + 1) * 128, :] = rows.astype(BF16)

    def send_rows(n):
        ry = lax.rem(y + n + 1, 4)
        rows = pl.ds(pl.multiple_of(ry * 384, 384), 384)
        block = jnp.dot(T[rows, :], Wk[...], preferred_element_type=F32)
        ws[pl.ds(ry * 4, 4)] = block.astype(BF16).reshape(4, 4 * CAP, H)
        for m in range(4):
            p = ry * 4 + lax.rem(x + m, 4)
            if n == 3 and m == 0:
                pltpu.make_async_copy(ws.at[own], wr.at[own], loc.at[8]).start()
            else:
                w_copy(lax.rem(p - own + 16, 16), p).start()

    def build_TT():
        slot = lax.broadcasted_iota(jnp.int32, (128, EXPERTS * CAP), 1).astype(F32)
        for n in range(8):
            hit = slot == tgc[:, n : n + 1]
            TT[n * 128 : (n + 1) * 128, :] = jnp.where(hit, 1.0, 0.0).astype(BF16)

    def build_M2():
        lax.fori_loop(1, 16, pos_arrive, 0)
        pltpu.make_async_copy(ps.at[lax.div(own, 2)], posr.at[own], loc.at[3]).wait()
        odd = lax.rem(own, 2) == 1

        def one(b, carry):
            j = lax.broadcasted_iota(jnp.int32, (CAP, 128), 0).astype(F32)
            zero = jnp.zeros((CAP, 128), F32)
            first, second = (
                jnp.where(odd, part[4:8, :], part[0:4, :])
                for part in (posr[2 * b], posr[2 * b + 1])
            )
            rows = []
            for q in range(4):
                one_a = jnp.where(first[q : q + 1, :] == j, 1.0, 0.0)
                one_b = jnp.where(second[q : q + 1, :] == j, 1.0, 0.0)
                rows.append(jnp.concatenate([one_a, zero], axis=1))
                rows.append(jnp.concatenate([zero, one_b], axis=1))
            M2[b] = jnp.concatenate(rows, axis=0).astype(BF16)
            return carry

        lax.fori_loop(0, 8, one, 0)

    def build_wT():
        lax.fori_loop(1, 16, w_arrive, 0)
        pltpu.make_async_copy(ws.at[own], wr.at[own], loc.at[8]).wait()

        def one(s, carry):
            block = wr[s].astype(F32)
            for q in range(4):
                G[q // 2, pl.ds(q % 2 * H + s * CAP, CAP), 0:H] = block[q * CAP : (q + 1) * CAP, :]
            return carry

        lax.fori_loop(0, 16, one, 0)
        for q in range(4):
            wT[q] = jnp.transpose(G[q // 2, q % 2 * H : q % 2 * H + H, 0:H]).astype(BF16)

    def rows_of(c):
        g_wait(c, 3)

        def one(b, carry):
            block = cot[lax.div(b, 2), pl.ds(lax.rem(b, 2) * 2, 2), c].reshape(256, CW)
            got = jnp.dot(M2[b], block, preferred_element_type=F32).astype(BF16)
            for e in range(4):
                dsl[e // 2, pl.ds(e % 2 * H + b * 48, 48), :] = got[e * 48 : (e + 1) * 48, :]
            return carry

        lax.fori_loop(0, 8, one, 0)

    def partials(c):
        for e in range(4):
            got = jnp.dot(
                wT[e], dsl[e // 2, e % 2 * H : e % 2 * H + H, :], preferred_element_type=F32).astype(BF16)
            for s in range(8):
                Pb[c, s % 2, (e // 2) * 4 + s // 2, e % 2] = got[s * 48 : (s + 1) * 48, :]
        pair_copy(c).start()

    def hidden_grads(c):
        chain_end(c)
        for e in range(4):
            rows = slice(e % 2 * H, e % 2 * H + H)
            got = lax.dot_general(
                dsl[e // 2, rows, :],
                sec[e // 2, c].reshape(2 * H, CW),
                (((1,), (1,)), ((), ())),
                preferred_element_type=F32,
            )
            G[e // 2, rows, :] = got if c == 0 else G[e // 2, rows, :] + got

    def pair_copy(c):
        return remote(Pb.at[c, 1 - k], Ps.at[c], pd_s.at[c], pd_r.at[c], sib)

    def ring_copy(c, t, way):
        far = 4 - t
        d = lax.rem(z + far, 8) if way == 0 else lax.rem(z + 8 - far, 8)
        where = dzp if way == 0 else dzm
        if t == 0:
            src, dst = Pb.at[c, k, d, way], Rr.at[c, t, way, way]
        else:
            src, dst = Pb.at[c, k, d], Rr.at[c, t, way]
        return remote(src, dst, rs_s.at[c, t, way], rs_r.at[c, t, way], where)

    def pair_sum(c):
        pair_copy(c).wait_recv()
        Pb[c, k] = (Pb[c, k].astype(F32) + Ps[c].astype(F32)).astype(BF16)
        ring_copy(c, 0, 0).start()
        ring_copy(c, 0, 1).start()

    def ring_step(c, t):
        for way in range(2):
            far = 4 - t
            d = lax.rem(z + far, 8) if way == 0 else lax.rem(z + 8 - far, 8)
            ring_copy(c, t - 1, way).wait_recv()
            if t == 1:
                Pb[c, k, d, way] = (
                    Pb[c, k, d, way].astype(F32) + Rr[c, 0, way, way].astype(F32)
                ).astype(BF16)
            else:
                Pb[c, k, d] = (Pb[c, k, d].astype(F32) + Rr[c, t - 1, way].astype(F32)).astype(BF16)
            ring_copy(c, t, way).start()

    def z_copy(c, way, j):
        shard = jnp.maximum(zl - j, 0) if way == 0 else jnp.minimum(zl + j, 3)
        ref = nsx.at[c, 2 * shard + k]
        return remote(ref, ref, z_s.at[c, way, j], z_r.at[c, way, j], (dzp, dzm)[way])

    def z_sends(way, j):
        return ((zl >= j) & (zl < 3)) if way == 0 else ((zl + j <= 3) & (zl > 0))

    def y_copy(c, shard):
        ref = nsx.at[c, 2 * shard + k]
        return remote(ref, ref, y_s.at[c, shard], y_r.at[c, shard], sib)

    def ns_out(c):
        return pltpu.make_async_copy(nsx.at[c], ns.at[:, :, :, cols(c)], out_s.at[c])

    def out_copies(c):
        q = cols(c)
        return [
            pltpu.make_async_copy(v.at[:, :, q], dst.at[:, :, q], loc.at[9 + 3 * c + n])
            for n, (v, dst) in enumerate(((wv, nw), (m1v, nm1), (m2v, nm2)))
        ]

    def adam(c):
        q = cols(c)
        if c == 0:
            for cp in locals_[1:]:
                cp.wait()
        ring_copy(c, 3, 0).wait_recv()
        ring_copy(c, 3, 1).wait_recv()
        for e in range(2):
            grad = Pb[c, k, z, e].astype(F32) + Rr[c, 3, 0, e].astype(F32)
            grad = grad + Rr[c, 3, 1, e].astype(F32)
            w = wv[:, e, q]
            a = beta_one * m1v[:, e, q] + (1.0 - beta_one) * grad
            b = beta_two * m2v[:, e, q] + (1.0 - beta_two) * grad * grad
            update = a / bias_one / (jnp.sqrt(b / bias_two) + adam_epsilon) + decay_rate * w
            wv[:, e, q] = w - learn_rate * update
            m1v[:, e, q] = a
            m2v[:, e, q] = b
        nsx[c, 2 * zl + k] = wv[:, :, q].astype(BF16)
        for way in range(2):
            pl.when(z_sends(way, 0))(z_copy(c, way, 0).start)
        y_copy(c, zl).start()
        for cp in out_copies(c):
            cp.start()

    def z_forward(c, j):
        for way in range(2):
            shard = zl - j if way == 0 else zl + j

            @pl.when((shard >= 0) & (shard < 4))
            def _():
                z_copy(c, way, j - 1).wait_recv()
                if j < 3:
                    pl.when(z_sends(way, j))(z_copy(c, way, j).start)
                y_copy(c, shard).start()

    def z_end(c):
        for shard in range(4):
            y_copy(c, shard).wait_recv()
        ns_out(c).start()

    def send_back():
        at = lax.broadcasted_iota(jnp.int32, (2 * H, H), 0)
        column = lax.broadcasted_iota(jnp.int32, (2 * H, H), 1)
        for e in range(4):
            rows = slice(e % 2 * H, e % 2 * H + H)
            pick = jnp.where(at == 2 * column + e % 2, 1.0, 0.0).astype(BF16)
            G[e // 2, rows, 0:H] = jnp.dot(
                G[e // 2, rows, :].astype(BF16), pick, preferred_element_type=F32
            )

        def one(r, carry):
            s = lax.rem(own + r, 16)
            rows = [G[e // 2, pl.ds(e % 2 * H + s * CAP, CAP), 0:H] for e in range(4)]
            bs[s] = jnp.concatenate(rows, axis=0).astype(BF16)

            @pl.when(r < 16)
            def _():
                back_copy(r, s).start()

            return carry

        lax.fori_loop(1, 17, one, 0)
        pltpu.make_async_copy(bs.at[own], br.at[own], loc.at[7]).start()

    def finish():
        pltpu.make_async_copy(bs.at[own], br.at[own], loc.at[7]).wait()

        def arrive(r, carry):
            p = lax.rem(own + 16 - r, 16)
            remote(br.at[p], br.at[p], b_s.at[r], b_r.at[r], plane(p)).wait_recv()
            return carry

        lax.fori_loop(1, 16, arrive, 0)

        probs_out = []
        for n in range(8):
            g = jnp.dot(
                TT[n * 128 : (n + 1) * 128, :],
                br[...].reshape(EXPERTS * CAP, H),
                preferred_element_type=F32,
            )
            outf[:, n, :] = pc[:, n : n + 1] * g
            probs_out.append(jnp.sum(hid[:, n, :].astype(F32) * g, axis=1, keepdims=True))
        dpT[...] = jnp.transpose(jnp.concatenate(probs_out, axis=1))
        dh[...] = outf[...].astype(BF16)

    def pos_arrive(r, carry):
        p = lax.rem(own + 16 - r, 16)
        remote(posr.at[p], posr.at[p], pos_s.at[r], pos_r.at[r], plane(p)).wait_recv()
        return carry

    def w_arrive(r, carry):
        p = lax.rem(own + 16 - r, 16)
        remote(wr.at[p], wr.at[p], w_s.at[r], w_r.at[r], plane(p)).wait_recv()
        return carry

    g_start(0, 0)
    chain_begin(0)
    chain_begin(1)
    chain_begin(2)
    chain_begin(3)
    chain_begin(4)
    chain_begin(5)
    chain_begin(6)
    g_wait(0, 0)
    g_start(0, 1)
    chain_begin(7)
    choices()
    g_wait(0, 1)
    g_start(0, 2)
    build_rows()
    chain_step(0)
    send_rows(0)
    send_rows(1)
    send_rows(2)
    chain_step(1)
    send_rows(3)
    g_start(1, 0)
    g_start(2, 0)
    g_start(3, 0)
    g_start(4, 0)
    g_wait(0, 2)
    g_start(0, 3)
    build_M2()
    chain_step(2)
    build_TT()
    chain_step(3)
    chain_step(4)
    chain_step(5)
    g_wait(1, 0)
    g_start(1, 1)
    build_wT()
    g_wait(2, 0)
    g_start(2, 1)
    chain_step(6)
    g_wait(3, 0)
    g_start(3, 1)
    g_wait(4, 0)
    g_start(4, 1)
    g_wait(1, 1)
    g_start(1, 2)
    rows_of(0)
    g_wait(2, 1)
    g_start(2, 2)
    g_start(5, 0)
    partials(0)
    chain_step(7)
    hidden_grads(0)
    g_wait(1, 2)
    g_start(1, 3)
    g_wait(3, 1)
    g_start(3, 2)
    pair_sum(0)
    chain_step(8)
    g_wait(2, 2)
    g_start(2, 3)
    g_wait(4, 1)
    g_start(4, 2)
    ring_step(0, 1)
    g_wait(5, 0)
    g_start(5, 1)
    rows_of(1)
    chain_step(9)
    g_start(6, 0)
    partials(1)
    ring_step(0, 2)
    g_wait(3, 2)
    g_start(3, 3)
    hidden_grads(1)
    chain_step(10)
    rows_of(2)
    pair_sum(1)
    ring_step(0, 3)
    g_start(7, 0)
    g_wait(5, 1)
    g_start(5, 2)
    g_wait(4, 2)
    g_start(4, 3)
    g_wait(6, 0)
    g_start(6, 1)
    partials(2)
    ring_step(1, 1)
    hidden_grads(2)
    g_wait(7, 0)
    g_start(7, 1)
    adam(0)
    pair_sum(2)
    ring_step(1, 2)
    rows_of(3)
    g_wait(5, 2)
    g_start(5, 3)
    z_forward(0, 1)
    g_wait(6, 1)
    g_start(6, 2)
    g_wait(7, 1)
    g_start(7, 2)
    ring_step(2, 1)
    ring_step(1, 3)
    partials(3)
    z_forward(0, 2)
    hidden_grads(3)
    ring_step(2, 2)
    rows_of(4)
    pair_sum(3)
    g_wait(6, 2)
    g_start(6, 3)
    z_forward(0, 3)
    adam(1)
    ring_step(2, 3)
    ring_step(3, 1)
    g_wait(7, 2)
    g_start(7, 3)
    partials(4)
    z_forward(1, 1)
    hidden_grads(4)
    adam(2)
    pair_sum(4)
    ring_step(3, 2)
    rows_of(5)
    z_forward(1, 2)
    z_forward(2, 1)
    ring_step(4, 1)
    partials(5)
    ring_step(3, 3)
    hidden_grads(5)
    z_forward(1, 3)
    rows_of(6)
    pair_sum(5)
    ring_step(4, 2)
    z_forward(2, 2)
    adam(3)
    partials(6)
    ring_step(5, 1)
    ring_step(4, 3)
    hidden_grads(6)
    z_forward(2, 3)
    rows_of(7)
    pair_sum(6)
    ring_step(5, 2)
    z_forward(3, 1)
    partials(7)
    adam(4)
    ring_step(6, 1)
    ring_step(5, 3)
    hidden_grads(7)
    pair_sum(7)
    z_forward(3, 2)
    z_forward(4, 1)
    send_back()
    ring_step(6, 2)
    ring_step(7, 1)
    adam(5)
    z_forward(3, 3)
    z_end(0)
    z_forward(4, 2)
    z_end(1)
    z_end(2)
    ring_step(6, 3)
    z_end(3)
    ring_step(7, 2)
    z_forward(5, 1)
    z_forward(4, 3)
    adam(6)
    z_end(4)
    ring_step(7, 3)
    z_forward(5, 2)
    z_forward(6, 1)
    adam(7)
    z_forward(5, 3)
    z_forward(6, 2)
    z_end(5)
    z_forward(7, 1)
    z_forward(6, 3)
    z_forward(7, 2)
    z_end(6)
    finish()
    z_forward(7, 3)
    z_end(7)

    def sent(r, carry):
        p = lax.rem(own + r, 16)
        pos_copy(r, p).wait_send()
        w_copy(r, p).wait_send()
        back_copy(r, p).wait_send()
        return carry

    lax.fori_loop(1, 16, sent, 0)
    for c in range(NC):
        for n in range(16):
            gather_send(c, n).wait_send()
        for way in range(2):
            chain_sib(c, way).wait_send()
            for t in range(4):
                ring_copy(c, t, way).wait_send()
        chain(c, 0).wait_send()
        chain(c, 1).wait_send()
        pair_copy(c).wait_send()
        for way in range(2):
            for j in range(3):
                pl.when(z_sends(way, j))(z_copy(c, way, j).wait_send)
        for shard in range(4):
            y_copy(c, shard).wait_send()
        ns_out(c).wait()
        for cp in out_copies(c):
            cp.wait()


def local(cotangent, hidden, probs, expert_ids, secondary, weight, moment1, moment2):
    hbm = pl.BlockSpec(memory_space=pl.ANY)
    vmem = pl.BlockSpec(memory_space=pltpu.VMEM)
    dma = pltpu.SemaphoreType.DMA
    shape = jax.ShapeDtypeStruct
    dh, dpT, nw, nm1, nm2, ns = pl.pallas_call(
        body,
        out_shape=(
            shape((128, 8, H), BF16),
            shape((8, 128), F32),
            shape((48, 2, D), F32),
            shape((48, 2, D), F32),
            shape((48, 2, D), F32),
            shape((8, 48, 2, D), BF16),
        ),
        in_specs=[hbm, vmem, vmem] + [hbm] * 5,
        out_specs=(vmem, vmem, hbm, hbm, hbm, hbm),
        scratch_shapes=[
            pltpu.VMEM((4, 4, NC, 128, CW), BF16),
            pltpu.VMEM((2, NC, H, 2, CW), BF16),
            pltpu.VMEM((8, 8, 128), F32),
            pltpu.VMEM((16, 8, 128), F32),
            pltpu.VMEM((16, 4 * CAP, H), BF16),
            pltpu.VMEM((16, 4 * CAP, H), BF16),
            pltpu.VMEM((2, 2 * H, 2 * H), F32),
            pltpu.VMEM((4, H, H), BF16),
            pltpu.VMEM((8, 192, 256), BF16),
            pltpu.VMEM((2, 2 * H, CW), BF16),
            pltpu.VMEM((NC, 2, 8, 2, 48, CW), BF16),
            pltpu.VMEM((NC, 8, 2, 48, CW), BF16),
            pltpu.VMEM((NC, 4, 2, 2, 48, CW), BF16),
            pltpu.VMEM((16, 4 * CAP, H), BF16),
            pltpu.VMEM((16, 4 * CAP, H), BF16),
            pltpu.VMEM((1024, EXPERTS * CAP), BF16),
            pltpu.VMEM((EXPERTS * CAP, 1024), BF16),
            pltpu.VMEM((1024, H), BF16),
            pltpu.VMEM((128, 8, H), BF16),
            pltpu.VMEM((128, 8, H), F32),
            pltpu.VMEM((8, 128), F32),
            pltpu.VMEM((128, 8), F32),
            pltpu.VMEM((128, 8), F32),
            pltpu.VMEM((48, 2, D), F32),
            pltpu.VMEM((48, 2, D), F32),
            pltpu.VMEM((48, 2, D), F32),
            pltpu.VMEM((NC, 8, 48, 2, CW), BF16),
            dma((9 + 3 * NC,)), dma((2, NC)), dma((NC,)),
            dma((16,)), dma((16,)), dma((16,)), dma((16,)), dma((16,)), dma((16,)),
            dma((NC, 16)), dma((NC, 16)),
            dma((NC, 2)), dma((NC, 2)), dma((NC, 2)), dma((NC, 2)),
            dma((NC,)), dma((NC,)),
            dma((NC, 4, 2)), dma((NC, 4, 2)),
            dma((NC, 2, 3)), dma((NC, 2, 3)), dma((NC, 4)), dma((NC, 4)),
        ],
        compiler_params=pltpu.CompilerParams(
            collective_id=0, has_side_effects=True, vmem_limit_bytes=60 * 1024 * 1024
        ),
    )(cotangent, expert_ids.T, probs.T, hidden, secondary, weight, moment1, moment2)
    return dh, dpT.T, nw, nm1, nm2, ns.reshape(H, 2, D)


def solution(mesh):
    in_specs = (
        P(("outer", "inner"), None),
        P(("outer", "inner"), None, None),
        P(("outer", "inner"), None),
        P(("outer", "inner"), None),
        P(None, "inner", None),
        P("outer", "inner", None),
        P("outer", "inner", None),
        P("outer", "inner", None),
    )
    out_specs = (
        P(("outer", "inner"), None, None),
        P(("outer", "inner"), None),
        P("outer", "inner", None),
        P("outer", "inner", None),
        P("outer", "inner", None),
        P(None, "inner", None),
    )
    return jax.shard_map(local, mesh=mesh, in_specs=in_specs, out_specs=out_specs, check_vma=False)
```

time: 276 us -> 150 us (0.54)
  Pallas kernels: 246 us -> 141 us
  local copies, waits for them, and re-layouts: 23.7 us -> 9.02 us
  matrix products: 3 us -> 0 us
  other arithmetic: 2.94 us -> 0 us
    pallas_call x1, Pallas kernels: 246 us -> 141 us  [local(): pl.pallas_call(body, out_shape=(shape((128, 8, H), BF16), shape((8, 128),...]
    unnamed x25 -> x12, local copies, waits for them, and re-layouts: 18.5 us -> 9.02 us
    dot_general x2 -> x0, matrix products: 3 us -> none  [the longest x1 2.91 us: local(): wsend = jnp.dot(matches, weighted, preferred_element_type=F32).astype(BF16)]
where the time goes in v2:
time: 150 us
  Pallas kernels  141 us (94%)
  local copies, waits for them, and re-layouts  9.02 us (6%)
    pallas_call x1, Pallas kernels, local(): pl.pallas_call(body, out_shape=(shape((128, 8, H), BF16), shape((8, 128),...  141 us
    unnamed x12, local copies, waits for them, and re-layouts  9.02 us

profile of v2, /device:TPU:1, one launch (start us, length us, event | category | flops | bytes accessed | tf_op | source)
XLA Modules:
  0.0 150.2 jit_solution(14792188424479515914)
XLA Ops:
  0.6 140.5 %shard_map.127 = (bf16[128,8,384]{2,1,0:T(8,128)(2,1)}, f32[8,128]{1,0:T(8,128)}, f32[48,2,2048]{2,1,0:T(2,128)}, f32[48,2,2048]{2,1,0:T(2,128)}, f32[48,2,2048]...) custom-call(bf16[128,2048]{1,0:T(8,128)(2,1)} %cot_hbm.1, s32[8,128]{1,0:T(8,128)} %bitcast.6, f32[8,128]{1,0:T(8,128)} %bitcast.7, ...), custom_call_target="tpu_custom_call" | custom-call | tf_op jit(solution)/shard_map/pallas_call | solution.py:693
  141.2 0.0 copy-start.2
  141.2 0.0 copy-start.1
  141.2 0.0 copy-start
  141.2 2.2 %copy.20 = bf16[128,8,384]{2,1,0:T(8,128)(2,1)} copy(bf16[128,8,384]{2,1,0:T(8,128)(2,1)} %get-tuple-element.24) | data formatting | bytes 1572864
  143.4 1.3 copy.21
  144.7 2.1 %copy.22 = f32[48,2,2048]{2,1,0:T(2,128)} copy(f32[48,2,2048]{2,1,0:T(2,128)} %get-tuple-element.26) | data formatting | bytes 1572864
  146.8 0.0 copy-done.2
  146.8 0.9 copy.23
  147.7 0.0 copy-done.1
  147.7 0.9 copy.24
  148.5 0.0 copy-done
  148.6 1.7 %copy.25 = bf16[384,2,2048]{2,1,0:T(2,128)(2,1)} copy(bf16[384,2,2048]{2,1,0:T(2,128)(2,1)S(1)} %bitcast.4) | data formatting | bytes 6291456
Async XLA Ops:
  141.2 5.6 %copy-start.2 = (f32[48,2,2048]{2,1,0:T(2,128)S(1)}, f32[48,2,2048]{2,1,0:T(2,128)}, u32[]{:S(2)}) copy-start(f32[48,2,2048]{2,1,0:T(2,128)} %get-tuple-element.27) | copy-start | bytes 2359300
  141.2 6.5 %copy-start.1 = (f32[48,2,2048]{2,1,0:T(2,128)S(1)}, f32[48,2,2048]{2,1,0:T(2,128)}, u32[]{:S(2)}) copy-start(f32[48,2,2048]{2,1,0:T(2,128)} %get-tuple-element.28) | copy-start | bytes 2359300
  141.2 7.4 %copy-start = (bf16[8,48,2,2048]{3,2,1,0:T(2,128)(2,1)S(1)}, bf16[8,48,2,2048]{3,2,1,0:T(2,128)(2,1)}, u32[]{:S(2)}) copy-start(bf16[8,48,2,2048]{3,2,1,0:T(2,128)(2,1)} %get-tuple-element.17) | copy-start | bytes 9437188

commit v3 on v2

--- a/solution.py
+++ b/solution.py
@@ -11,7 +11,7 @@
 CAP = 24
 H = 384
 D = 2048
-NC = 8
+NC = 4
 CW = D // NC
 MESH = pl.DeviceIdType.MESH
 F32 = jnp.float32
@@ -417,6 +417,35 @@
         for shard in range(4):
             y_copy(c, shard).wait_recv()
         ns_out(c).start()
+        for way in range(2):
+            for t in range(4):
+                ring_copy(c, t, way).wait_send()
+            for j in range(3):
+                pl.when(z_sends(way, j))(z_copy(c, way, j).wait_send)
+        pair_copy(c).wait_send()
+        for shard in range(4):
+            y_copy(c, shard).wait_send()
+        for cp in out_copies(c):
+            cp.wait()
+
+    def back_sent(r, carry):
+        back_copy(r, lax.rem(own + r, 16)).wait_send()
+        return carry
+
+    def early_sent():
+        def one(r, carry):
+            p = lax.rem(own + r, 16)
+            pos_copy(r, p).wait_send()
+            w_copy(r, p).wait_send()
+            return carry
+
+        lax.fori_loop(1, 16, one, 0)
+        for c in range(NC):
+            for n in range(16):
+                gather_send(c, n).wait_send()
+            for way in range(2):
+                chain_sib(c, way).wait_send()
+                chain(c, way).wait_send()
 
     def send_back():
         at = lax.broadcasted_iota(jnp.int32, (2 * H, H), 0)
@@ -474,215 +503,109 @@
         remote(wr.at[p], wr.at[p], w_s.at[r], w_r.at[r], plane(p)).wait_recv()
         return carry
 
-    g_start(0, 0)
     chain_begin(0)
     chain_begin(1)
     chain_begin(2)
     chain_begin(3)
-    chain_begin(4)
-    chain_begin(5)
-    chain_begin(6)
+    g_start(0, 0)
+    choices()
     g_wait(0, 0)
     g_start(0, 1)
-    chain_begin(7)
-    choices()
+    build_TT()
+    chain_step(0)
     g_wait(0, 1)
     g_start(0, 2)
     build_rows()
-    chain_step(0)
     send_rows(0)
     send_rows(1)
     send_rows(2)
     chain_step(1)
     send_rows(3)
     g_start(1, 0)
-    g_start(2, 0)
-    g_start(3, 0)
-    g_start(4, 0)
     g_wait(0, 2)
     g_start(0, 3)
+    g_start(2, 0)
     build_M2()
     chain_step(2)
-    build_TT()
     chain_step(3)
-    chain_step(4)
-    chain_step(5)
+    build_wT()
     g_wait(1, 0)
     g_start(1, 1)
-    build_wT()
+    chain_step(4)
+    rows_of(0)
+    g_wait(1, 1)
+    g_start(1, 2)
+    partials(0)
     g_wait(2, 0)
     g_start(2, 1)
+    chain_step(5)
+    g_start(3, 0)
+    hidden_grads(0)
+    pair_sum(0)
+    g_wait(1, 2)
+    g_start(1, 3)
+    g_wait(2, 1)
+    g_start(2, 2)
     chain_step(6)
     g_wait(3, 0)
     g_start(3, 1)
-    g_wait(4, 0)
-    g_start(4, 1)
-    g_wait(1, 1)
-    g_start(1, 2)
-    rows_of(0)
-    g_wait(2, 1)
-    g_start(2, 2)
-    g_start(5, 0)
-    partials(0)
-    chain_step(7)
-    hidden_grads(0)
-    g_wait(1, 2)
-    g_start(1, 3)
+    ring_step(0, 1)
+    rows_of(1)
+    partials(1)
+    hidden_grads(1)
     g_wait(3, 1)
     g_start(3, 2)
-    pair_sum(0)
-    chain_step(8)
+    ring_step(0, 2)
     g_wait(2, 2)
     g_start(2, 3)
-    g_wait(4, 1)
-    g_start(4, 2)
-    ring_step(0, 1)
-    g_wait(5, 0)
-    g_start(5, 1)
-    rows_of(1)
-    chain_step(9)
-    g_start(6, 0)
-    partials(1)
-    ring_step(0, 2)
+    pair_sum(1)
+    ring_step(0, 3)
+    ring_step(1, 1)
     g_wait(3, 2)
     g_start(3, 3)
-    hidden_grads(1)
-    chain_step(10)
+    adam(0)
     rows_of(2)
-    pair_sum(1)
-    ring_step(0, 3)
-    g_start(7, 0)
-    g_wait(5, 1)
-    g_start(5, 2)
-    g_wait(4, 2)
-    g_start(4, 3)
-    g_wait(6, 0)
-    g_start(6, 1)
+    ring_step(1, 2)
     partials(2)
-    ring_step(1, 1)
+    z_forward(0, 1)
     hidden_grads(2)
-    g_wait(7, 0)
-    g_start(7, 1)
-    adam(0)
-    pair_sum(2)
-    ring_step(1, 2)
+    ring_step(1, 3)
     rows_of(3)
-    g_wait(5, 2)
-    g_start(5, 3)
-    z_forward(0, 1)
-    g_wait(6, 1)
-    g_start(6, 2)
-    g_wait(7, 1)
-    g_start(7, 2)
-    ring_step(2, 1)
-    ring_step(1, 3)
     partials(3)
     z_forward(0, 2)
+    pair_sum(2)
+    adam(1)
     hidden_grads(3)
+    ring_step(2, 1)
+    z_forward(0, 3)
+    pair_sum(3)
+    z_forward(1, 1)
+    send_back()
     ring_step(2, 2)
-    rows_of(4)
-    pair_sum(3)
-    g_wait(6, 2)
-    g_start(6, 3)
-    z_forward(0, 3)
-    adam(1)
+    ring_step(3, 1)
+    z_end(0)
+    z_forward(1, 2)
     ring_step(2, 3)
-    ring_step(3, 1)
-    g_wait(7, 2)
-    g_start(7, 3)
-    partials(4)
-    z_forward(1, 1)
-    hidden_grads(4)
+    ring_step(3, 2)
+    z_forward(1, 3)
+    z_end(1)
     adam(2)
-    pair_sum(4)
-    ring_step(3, 2)
-    rows_of(5)
-    z_forward(1, 2)
+    ring_step(3, 3)
     z_forward(2, 1)
-    ring_step(4, 1)
-    partials(5)
-    ring_step(3, 3)
-    hidden_grads(5)
-    z_forward(1, 3)
-    rows_of(6)
-    pair_sum(5)
-    ring_step(4, 2)
+    adam(3)
+    early_sent()
+    finish()
     z_forward(2, 2)
-    adam(3)
-    partials(6)
-    ring_step(5, 1)
-    ring_step(4, 3)
-    hidden_grads(6)
+    z_forward(3, 1)
     z_forward(2, 3)
-    rows_of(7)
-    pair_sum(6)
-    ring_step(5, 2)
-    z_forward(3, 1)
-    partials(7)
-    adam(4)
-    ring_step(6, 1)
-    ring_step(5, 3)
-    hidden_grads(7)
-    pair_sum(7)
+    z_end(2)
     z_forward(3, 2)
-    z_forward(4, 1)
-    send_back()
-    ring_step(6, 2)
-    ring_step(7, 1)
-    adam(5)
     z_forward(3, 3)
-    z_end(0)
-    z_forward(4, 2)
-    z_end(1)
-    z_end(2)
-    ring_step(6, 3)
     z_end(3)
-    ring_step(7, 2)
-    z_forward(5, 1)
-    z_forward(4, 3)
-    adam(6)
-    z_end(4)
-    ring_step(7, 3)
-    z_forward(5, 2)
-    z_forward(6, 1)
-    adam(7)
-    z_forward(5, 3)
-    z_forward(6, 2)
-    z_end(5)
-    z_forward(7, 1)
-    z_forward(6, 3)
-    z_forward(7, 2)
-    z_end(6)
-    finish()
-    z_forward(7, 3)
-    z_end(7)
-
-    def sent(r, carry):
-        p = lax.rem(own + r, 16)
-        pos_copy(r, p).wait_send()
-        w_copy(r, p).wait_send()
-        back_copy(r, p).wait_send()
-        return carry
-
-    lax.fori_loop(1, 16, sent, 0)
+
+    lax.fori_loop(1, 16, back_sent, 0)
     for c in range(NC):
-        for n in range(16):
-            gather_send(c, n).wait_send()
-        for way in range(2):
-            chain_sib(c, way).wait_send()
-            for t in range(4):
-                ring_copy(c, t, way).wait_send()
-        chain(c, 0).wait_send()
-        chain(c, 1).wait_send()
-        pair_copy(c).wait_send()
-        for way in range(2):
-            for j in range(3):
-                pl.when(z_sends(way, j))(z_copy(c, way, j).wait_send)
-        for shard in range(4):
-            y_copy(c, shard).wait_send()
         ns_out(c).wait()
-        for cp in out_copies(c):
-            cp.wait()
 
 
 def local(cotangent, hidden, probs, expert_ids, secondary, weight, moment1, moment2):

time: 150 us -> 143 us (0.953)
  Pallas kernels: 141 us -> 133 us
    pallas_call x1, Pallas kernels: 141 us -> 133 us  [local(): pl.pallas_call(body, out_shape=(shape((128, 8, H), BF16), shape((8, 128),...]
where the time goes in v3:
time: 143 us
  Pallas kernels  133 us (93%)
  local copies, waits for them, and re-layouts  9.02 us (6%)
    pallas_call x1, Pallas kernels, local(): pl.pallas_call(body, out_shape=(shape((128, 8, H), BF16), shape((8, 128),...  133 us
    unnamed x12, local copies, waits for them, and re-layouts  9.02 us

profile of v3, /device:TPU:1, one launch (start us, length us, event | category | flops | bytes accessed | tf_op | source)
XLA Modules:
  0.0 142.5 jit_solution(1980286369724064881)
XLA Ops:
  0.6 132.9 %shard_map.127 = (bf16[128,8,384]{2,1,0:T(8,128)(2,1)}, f32[8,128]{1,0:T(8,128)}, f32[48,2,2048]{2,1,0:T(2,128)}, f32[48,2,2048]{2,1,0:T(2,128)}, f32[48,2,2048]...) custom-call(bf16[128,2048]{1,0:T(8,128)(2,1)} %cot_hbm.1, s32[8,128]{1,0:T(8,128)} %bitcast.6, f32[8,128]{1,0:T(8,128)} %bitcast.7, ...), custom_call_target="tpu_custom_call" | custom-call | tf_op jit(solution)/shard_map/pallas_call | solution.py:616
  133.5 0.0 copy-start.2
  133.5 0.0 copy-start.1
  133.5 0.0 copy-start
  133.5 2.2 %copy.20 = bf16[128,8,384]{2,1,0:T(8,128)(2,1)} copy(bf16[128,8,384]{2,1,0:T(8,128)(2,1)} %get-tuple-element.24) | data formatting | bytes 1572864
  135.8 1.3 copy.21
  137.0 2.1 %copy.22 = f32[48,2,2048]{2,1,0:T(2,128)} copy(f32[48,2,2048]{2,1,0:T(2,128)} %get-tuple-element.26) | data formatting | bytes 1572864
  139.1 0.0 copy-done.2
  139.1 0.9 copy.23
  140.0 0.0 copy-done.1
  140.0 0.9 copy.24
  140.9 0.0 copy-done
  140.9 1.7 %copy.25 = bf16[384,2,2048]{2,1,0:T(2,128)(2,1)} copy(bf16[384,2,2048]{2,1,0:T(2,128)(2,1)S(1)} %bitcast.4) | data formatting | bytes 6291456
Async XLA Ops:
  133.5 5.6 %copy-start.2 = (f32[48,2,2048]{2,1,0:T(2,128)S(1)}, f32[48,2,2048]{2,1,0:T(2,128)}, u32[]{:S(2)}) copy-start(f32[48,2,2048]{2,1,0:T(2,128)} %get-tuple-element.27) | copy-start | bytes 2359300
  133.5 6.5 %copy-start.1 = (f32[48,2,2048]{2,1,0:T(2,128)S(1)}, f32[48,2,2048]{2,1,0:T(2,128)}, u32[]{:S(2)}) copy-start(f32[48,2,2048]{2,1,0:T(2,128)} %get-tuple-element.28) | copy-start | bytes 2359300
  133.5 7.4 %copy-start = (bf16[8,48,2,2048]{3,2,1,0:T(2,128)(2,1)S(1)}, bf16[8,48,2,2048]{3,2,1,0:T(2,128)(2,1)}, u32[]{:S(2)}) copy-start(bf16[8,48,2,2048]{3,2,1,0:T(2,128)(2,1)} %get-tuple-element.17) | copy-start | bytes 9437188
